TPU v7x, 256 devices: a whole 4x4x8 slice. The times are simulated.
256 devices in a mesh: row: 16 (over z, core), blk: 16 (over y, x).
Axes of the slice: x: 4, y: 4, z: 8, core: 2. Of those that a mesh axis runs over, the one named last changes fastest.
Arguments:
- tiles: bfloat16 [16, 16, 32, 256, 256], P('row', 'blk')
- tile_rows: int32 [16, 16, 32], P('row', 'blk'), may hold values from 0 to 15, as said below
- tile_cols: int32 [16, 16, 32], P('row', 'blk'), may hold values from 0 to 3, as said below
- counts: int32 [16, 16], P('row', 'blk'), may hold values from 8 to 32, as said below
- sketch: bfloat16 [65536, 512], P(('row', 'blk')), may hold values from -6 to 6
Outputs:
- basis: float32 [65536, 512], P(('row', 'blk'))
- factor: float32 [512, 512], replicated
Inputs may be any that keep to these rules, and one draw needn't show every extreme that they name: In each row group and column group, all 32 slots name distinct pairs (tile_rows, tile_cols). `tile_cols`: see tile_rows: the pairs are distinct in every row group and column group. `counts`: some row group and column group uses all 32 slots.
All inputs are finite; a program needn't handle non-finite values.
Results may differ from a plain program's by a relative error of at most 0.0027.
Values may be sent and summed in bfloat16 or wider, within the bound.
A program may use at most 128 MiB of HBM per device.

v0:
```python
import jax
import jax.numpy as jnp
from jax import lax
from jax.sharding import PartitionSpec as P

RB = 16
CB = 4


def local(tiles, tile_rows, tile_cols, counts, sketch):
    high = lax.Precision.HIGHEST
    blocks = tiles[0, 0]
    row_ids = tile_rows[0, 0]
    col_ids = tile_cols[0, 0]
    filled = counts[0, 0]
    slots = blocks.shape[0]
    edge = blocks.shape[1]
    live = jnp.arange(slots) < filled
    placement_hot = (
        (row_ids[:, None, None] == jnp.arange(RB)[None, :, None])
        & (col_ids[:, None, None] == jnp.arange(CB)[None, None, :])
        & live[:, None, None]
    ).astype(jnp.bfloat16)
    dense = jnp.einsum("trc,tij->ricj", placement_hot, blocks, preferred_element_type=jnp.float32)
    dense = dense.astype(jnp.bfloat16).reshape(RB * edge, CB * edge)
    gathered = lax.all_gather(sketch, "blk", axis=0, tiled=True)
    partial_value = lax.dot_general(
        dense, gathered, (((0,), (0,)), ((), ())), preferred_element_type=jnp.float32
    )
    column_image = lax.psum(partial_value, "row").astype(jnp.bfloat16)
    image = lax.psum_scatter(
        jnp.dot(dense, column_image, preferred_element_type=jnp.float32),
        "blk",
        scatter_dimension=0,
        tiled=True,
    )
    total_rows = image.shape[0] * lax.axis_size("row") * lax.axis_size("blk")
    local_gram = jnp.dot(image.T, image, precision=high) / total_rows
    gram = lax.psum(local_gram, ("row", "blk"))
    lower = jnp.linalg.cholesky(gram)
    basis = lax.linalg.triangular_solve(lower, image, left_side=False, lower=True, transpose_a=True)
    return (basis, lower.T)


def solution(mesh):
    in_specs = (
        P("row", "blk", None, None, None),
        P("row", "blk", None),
        P("row", "blk", None),
        P("row", "blk"),
        P(("row", "blk"), None),
    )
    out_specs = (P(("row", "blk"), None), P())
    return jax.shard_map(local, mesh=mesh, in_specs=in_specs, out_specs=out_specs, check_vma=False)
```

profile of v0, /device:TPU:1, one launch (start us, length us, event | category | flops | bytes accessed | tf_op | source)
XLA Modules:
  0.0 651.9 jit_solution(14561657721721902896)
XLA Ops:
  7.2 0.7 all-gather.2.cloned.1.call-update
  8.6 0.7 iota_compare_fusion.4
  9.3 0.7 iota_compare_fusion.3
  9.9 8.3 %convert_bitcast_fusion = bf16[16,256,4,256]{3,0,1,2:T(8,128)(2,1)} fusion(bf16[32,256,256]{2,1,0:T(8,128)(2,1)} %bitcast.79, pred[32]{0:T(512)(128)(4,1)S(1)} %iota_compare_fusion.5, pred[32,4]{0,1:T(4,128)(4,1)S(1)} %iota_compare_fusion.4, pred[32,16]{0,1:T(8,128)(4,1)S(1)} %iota_compare_fusion.3), kind=kOutput, calls=%fused_computation.2 | convolution fusion | flops 272633856 | bytes 12583584 | tf_op jit(solution)/shard_map/trc,tij->ricj/dot_general | solution.py:24
  18.2 16.1 %copy.13 = bf16[16,256,4,256]{1,0,3,2:T(8,128)(2,1)} copy(bf16[16,256,4,256]{3,0,1,2:T(8,128)(2,1)} %convert_bitcast_fusion) | data formatting | bytes 16777216 | tf_op jit(solution)/shard_map/convert_element_type | solution.py:25
  34.3 12.3 %copy.20 = bf16[128,8,16,256]{3,1,2,0:T(8,128)(2,1)} copy(bf16[128,8,16,256]{3,2,1,0:T(8,128)(2,1)} %bitcast.76) | data formatting | bytes 16777216
  46.6 24.2 %all-gather.2.cloned.1.call-done = bf16[4096,512]{1,0:T(8,128)(2,1)} async-done(((bf16[256,512]{1,0:T(8,128)(2,1)}), bf16[4096,512]{1,0:T(8,128)(2,1)}) %all-gather.2.cloned.1.call-update) | async-done | bytes 4194320 | tf_op jit(solution)/shard_map/all_gather | solution.py:26
  70.8 8.1 %fusion.43 = f32[1024,512]{1,0:T(8,128)S(1)} fusion(bf16[4096,1024]{0,1:T(8,128)(2,1)} %bitcast.77, bf16[4096,512]{1,0:T(8,128)(2,1)} %all-gather.2.cloned.1.call-done), kind=kOutput, calls=%fused_computation.84 | convolution fusion | flops 4294967296 | bytes 14680064 | tf_op jit(solution)/shard_map/dot_general | solution.py:27
  79.0 58.2 %all-reduce.5 = bf16[1024,512]{1,0:T(8,128)(2,1)S(1)} all-reduce(f32[1024,512]{1,0:T(8,128)S(1)} %fusion.43), channel_id=1, replica_groups=mesh['row'=16,'blk'=16] {'row'}, use_global_device_ids=true, to_apply=%region_0.0 | all-reduce | flops 524288 | bytes 3145728 | tf_op jit(solution)/shard_map/psum | solution.py:30
  137.2 10.4 %fusion.44 = f32[4096,512]{1,0:T(8,128)} fusion(bf16[4096,1024]{0,1:T(8,128)(2,1)} %bitcast.78, bf16[1024,512]{1,0:T(8,128)(2,1)S(1)} %all-reduce.5), kind=kOutput, calls=%fused_computation.85 | convolution fusion | flops 4294967296 | bytes 17825792 | tf_op jit(solution)/shard_map/dot_general | solution.py:32
  147.6 88.9 %reduce-scatter.2.cloned.1.call-done = f32[256,512]{1,0:T(8,128)} async-done(((f32[4096,512]{1,0:T(8,128)}), f32[256,512]{1,0:T(8,128)}) %reduce-scatter.2.cloned.1.call-update) | async-done | bytes 524304 | tf_op jit(solution)/shard_map/reduce_scatter | solution.py:31
  236.5 3.3 convolution_multiply_fusion
  239.9 258.1 %all-reduce.4.cloned.1.call-done = f32[512,512]{0,1:T(8,128)} async-done(((f32[512,512]{0,1:T(8,128)}), f32[512,512]{0,1:T(8,128)}) %all-reduce.4.cloned.1.call-update) | async-done | bytes 1048592 | tf_op jit(solution)/shard_map/psum | solution.py:39
  498.0 1.6 copy.15
  499.5 1.4 fusion.2
  501.0 11.7 %cholesky.104 = f32[128,128]{1,0:T(8,128)S(1)} custom-call(f32[128,128]{1,0:T(8,128)S(1)} %cholesky.266), custom_call_target="Cholesky" | custom-call | tf_op jit(solution)/shard_map/jit(cholesky)/cholesky | solution.py:40
  512.8 9.8 %custom-call.30 = f32[1,128,128]{1,2,0:T(8,128)S(1)} custom-call(f32[1,128,128]{2,1,0:T(8,128)S(1)} %get-tuple-element.35), custom_call_target="InvertDiagBlocksLowerTriangular" | custom-call | tf_op jit(solution)/shard_map/jit(cholesky)/cholesky | solution.py:40
  523.0 0.3 convolution_subtract_fusion
  523.4 11.7 %cholesky.217 = f32[128,128]{1,0:T(8,128)S(1)} custom-call(f32[128,128]{1,0:T(8,128)S(1)} %cholesky.270), custom_call_target="Cholesky" | custom-call | tf_op jit(solution)/shard_map/jit(cholesky)/cholesky | solution.py:40
  535.3 9.8 %custom-call.31 = f32[1,128,128]{1,2,0:T(8,128)S(1)} custom-call(f32[1,128,128]{2,1,0:T(8,128)S(1)} %get-tuple-element.32), custom_call_target="InvertDiagBlocksLowerTriangular" | custom-call | tf_op jit(solution)/shard_map/jit(cholesky)/cholesky | solution.py:40
  545.4 0.4 convolution_subtract_fusion.3
  545.8 11.7 %cholesky.238 = f32[128,128]{1,0:T(8,128)S(1)} custom-call(f32[128,128]{1,0:T(8,128)S(1)} %cholesky.275), custom_call_target="Cholesky" | custom-call | tf_op jit(solution)/shard_map/jit(cholesky)/cholesky | solution.py:40
  557.6 0.7 compare_reduce_fusion.1
  558.3 9.8 %custom-call.32 = f32[1,128,128]{1,2,0:T(8,128)S(1)} custom-call(f32[1,128,128]{2,1,0:T(8,128)S(1)} %get-tuple-element.29), custom_call_target="InvertDiagBlocksLowerTriangular" | custom-call | tf_op jit(solution)/shard_map/jit(cholesky)/cholesky | solution.py:40
  568.3 0.4 convolution_subtract_fusion.5
  568.7 11.9 %cholesky.255 = f32[128,128]{1,0:T(8,128)S(1)} custom-call(f32[128,128]{1,0:T(8,128)S(1)} %convolution_subtract_fusion.5), custom_call_target="Cholesky" | custom-call | tf_op jit(solution)/shard_map/jit(cholesky)/cholesky | solution.py:40
  580.7 0.6 compare_reduce_fusion
  581.3 0.7 compare_reduce_fusion.2
  584.5 1.2 fusion.6
  585.7 11.7 %while.1 = (s32[]{:T(128)}, f32[512,512]{1,0:T(8,128)}, s32[4,2]{0,1:T(2,128)S(1)}, f32[4,128,128]{2,1,0:T(8,128)S(1)}, s32[]{:T(128)}) while((s32[]{:T(128)}, f32[512,512]{1,0:T(8,128)}, s32[4,2]{0,1:T(2,128)S(1)}, f32[4,128,128]{2,1,0:T(8,128)S(1)}, s32[]{:T(128)}) %tuple.34), condition=%wide.while_cond, body=%wide.while_body.sunk | while | flops 2 | bytes 131181 | solution.py:41
  585.8 0.6 fusion.57
  586.4 2.2 bitcast_dynamic-update-slice_fusion.2
  588.8 0.6 fusion.57
  589.4 2.2 bitcast_dynamic-update-slice_fusion.2
  591.7 0.6 fusion.57
  592.3 2.2 bitcast_dynamic-update-slice_fusion.2
  594.7 0.6 fusion.57
  595.3 2.2 bitcast_dynamic-update-slice_fusion.2
  597.5 39.3 %custom-call.33 = f32[4,128,128]{1,2,0:T(8,128)S(1)} custom-call(f32[4,128,128]{2,1,0:T(8,128)S(1)} %get-tuple-element.9), custom_call_target="InvertDiagBlocksLowerTriangular" | custom-call | tf_op jit(solution)/shard_map/triangular_solve | solution.py:41
  636.8 0.3 fusion.23
  637.1 1.2 convolution_subtract_fusion.4
  638.3 0.3 fusion.27
  638.7 1.5 convolution_subtract_fusion.2
  640.2 0.3 fusion.26
  640.5 1.8 convolution_subtract_fusion.1
  642.2 0.3 fusion.25
  642.6 1.0 copy.16
  643.6 1.3 copy.17
  (27 shorter events, 1.8 us)
Async XLA Ops:
  7.2 63.6 %all-gather.2.cloned.1.call-start = ((), (), s32[]{:S(2)}) async-start(), calls=%async_computation.1 | async-start | bytes 4456448 | tf_op jit(solution)/shard_map/all_gather | solution.py:26
  7.9 228.6 %reduce-scatter.2.cloned.1.call-start = ((), (), s32[]{:S(2)}) async-start(), calls=%async_computation.2 | async-start | bytes 8912896 | tf_op jit(solution)/shard_map/reduce_scatter | solution.py:31
  147.6 350.4 %all-reduce.4.cloned.1.call-start = ((), (), s32[]{:S(2)}) async-start(), calls=%async_computation.3 | async-start | bytes 2097152 | tf_op jit(solution)/shard_map/psum | solution.py:39
  236.5 400.2 %copy-start = (f32[256,512]{1,0:T(8,128)S(1)}, f32[256,512]{1,0:T(8,128)}, u32[]{:S(2)}) copy-start(f32[256,512]{1,0:T(8,128)} %reduce-scatter.2.cloned.1.call-done) | copy-start | bytes 1572868
Sparse Core Ops, SparseCore 0:
  10.4 60.3 all-gather.1
  147.7 88.7 reduce-scatter.1
  242.5 255.3 all-reduce.3
where the time goes:
time: 661 us; the launch traced here: 652 us
  waiting for transfers between devices  372 us (56%)
  other arithmetic  122 us (18%)
  blocking collectives  58.2 us (9%)
  local copies, waits for them, and re-layouts  44 us (7%)
  matrix products  37.7 us (6%)
  between operations  17.6 us (3%)
    psum x1, waiting for transfers between devices, local(): gram = lax.psum(local_gram, ('row', 'blk'))  258 us
    reduce_scatter x1, waiting for transfers between devices, local(): lax.psum_scatter(jnp.dot(dense, column_image, preferred_element_type=jnp....  88.9 us
    another operation x14, other arithmetic, local(): lower = jnp.linalg.cholesky(gram)  78.9 us
    psum x1, blocking collectives, local(): column_image = lax.psum(partial_value, 'row').astype(jnp.bfloat16)  58.2 us
    another operation x3, other arithmetic, local(): lax.linalg.triangular_solve(lower, image, left_side=False, lower=True, tr...  39.4 us
    all_gather x1, waiting for transfers between devices, local(): gathered = lax.all_gather(sketch, 'blk', axis=0, tiled=True)  24.2 us
    convert_element_type x1, local copies, waits for them, and re-layouts, local(): dense = dense.astype(jnp.bfloat16).reshape(RB * edge, CB * edge)  16.1 us
    unnamed x5, local copies, waits for them, and re-layouts  14.6 us
  transfers between devices with their start and end apart: 3, of which 3 were waited for; matrix products, arithmetic and copies ran while one was open for 6% of the time, Pallas kernels for 0%

commit v1 on v0

v1 whole, which is shorter than its diff:
```python
import functools
import jax
import jax.numpy as jnp
from jax import lax
from jax.experimental import pallas as pl
from jax.experimental.pallas import tpu as pltpu
from jax.sharding import PartitionSpec as P

F32 = jnp.float32
BF16 = jnp.bfloat16
MESH = pl.DeviceIdType.MESH
EDGE = 256
RB = 16
CB = 4
K = 512
PX, PY, PZ = 4, 4, 8


def where_am_i():
    row = lax.axis_index("row")
    blk = lax.axis_index("blk")
    return row // 2, row % 2, blk // PX, blk % PX


class Net:
    def __init__(self, send_sems, recv_sems):
        self.send_sems, self.recv_sems = send_sems, recv_sems
        self.used = 0
        self.z, self.c, self.y, self.x = where_am_i()

    def device(self, dz=0, dc=0, dy=0, dx=0):
        z = lax.rem(self.z + dz + PZ, PZ)
        c = 1 - self.c if dc else self.c
        y = lax.rem(self.y + dy + PY, PY)
        x = lax.rem(self.x + dx + PX, PX)
        return {"row": z * 2 + c, "blk": y * PX + x}

    def greet(self, steps):
        barrier = pltpu.get_barrier_semaphore()
        for step in steps:
            pl.semaphore_signal(barrier, inc=1, device_id=self.device(**step), device_id_type=MESH)
        pl.semaphore_wait(barrier, len(steps))

    def copy(self, src, dst, **step):
        slot = self.used
        self.used += 1
        return pltpu.make_async_remote_copy(
            src_ref=src, dst_ref=dst, send_sem=self.send_sems.at[slot], recv_sem=self.recv_sems.at[slot],
            device_id=self.device(**step), device_id_type=MESH)


NEIGHBOURS = [dict(dx=1), dict(dx=-1), dict(dy=1), dict(dy=-1), dict(dz=1), dict(dz=-1), dict(dc=1)]


def build_dense(slot_ref, tiles, dense):
    @pl.loop(0, RB)
    def _(i):
        for c in range(CB):
            slot = slot_ref[i * CB + c]
            keep = jnp.where(slot >= 0, 1.0, 0.0).astype(BF16)
            dense[i, :, c * EDGE:(c + 1) * EDGE] = tiles[jnp.maximum(slot, 0)] * keep


def column_kernel(slot_ref, tiles_hbm, sketch_ref, out, tiles, dense, gath, part, pair, chain, dma_sem, send_sems, recv_sems):
    net = Net(send_sems, recv_sems)
    load = pltpu.make_async_copy(tiles_hbm, tiles, dma_sem)
    load.start()
    mine = net.y * PX + net.x
    flipped = sketch_ref[...].astype(F32).T.astype(BF16)
    gath[mine] = flipped
    net.greet(NEIGHBOURS)
    started = []

    def start(copy):
        copy.start()
        started.append(copy)
        return copy

    half = EDGE
    axes = [("dx", "dy"), ("dy", "dx")]
    arrive = {}

    def slot_of(h, dp, dq):
        dx, dy = (dp, dq) if h == 0 else (dq, dp)
        return lax.rem(net.y + dy + PY, PY) * PX + lax.rem(net.x + dx + PX, PX)

    def push(h, dp, dq, axis, sign, key):
        where = gath.at[slot_of(h, dp, dq), pl.ds(h * half, half), :]
        arrive[key] = start(net.copy(where, where, **{axis: sign}))

    def received(h, dp, dq, key):
        where = gath.at[slot_of(h, dp, dq), pl.ds(h * half, half), :]
        slot = arrive[key]
        pltpu.make_async_remote_copy(
            src_ref=where, dst_ref=where, send_sem=slot_sem(key)[0], recv_sem=slot_sem(key)[1],
            device_id=net.device(dx=1), device_id_type=MESH).wait_recv()

    numbers = {}

    def slot_sem(key):
        return send_sems.at[numbers[key]], recv_sems.at[numbers[key]]

    def go(h, dp, dq, axis, sign, key):
        numbers[key] = net.used
        push(h, dp, dq, axis, sign, key)

    def multiply(h, dp, dq):
        block = gath[slot_of(h, dp, dq), h * half:(h + 1) * half, :]
        i = slot_of(h, dp, dq)
        for c in range(CB):
            prod = jnp.dot(block, dense[i, :, c * EDGE:(c + 1) * EDGE], preferred_element_type=F32)
            for s in range(2):
                rows = slice(h * half, (h + 1) * half)
                part[2 * c + s, rows, :] += prod[:, s * 128:(s + 1) * 128]

    for h in range(2):
        p, q = axes[h]
        go(h, 0, 0, p, 1, (h, -1, 0))
        go(h, 0, 0, p, -1, (h, 1, 0))
    for h in range(2):
        p, q = axes[h]
        go(h, 0, 0, q, 1, (h, 0, -1))
        go(h, 0, 0, q, -1, (h, 0, 1))
    load.wait()
    build_dense(slot_ref, tiles, dense)
    part[...] = jnp.zeros_like(part)
    for h in range(2):
        multiply(h, 0, 0)
    order = [(-1, 0), (1, 0), (0, -1), (0, 1), (2, 0), (-1, -1), (-1, 1), (0, 2), (1, -1), (1, 1), (-1, 2), (2, -1), (2, 1), (1, 2), (2, 2)]
    for dp, dq in order:
        for h in range(2):
            p, q = axes[h]
            received(h, dp, dq, (h, dp, dq))
            if dq == 0:
                if dp == -1:
                    go(h, dp, 0, p, 1, (h, 2, 0))
                go(h, dp, 0, q, 1, (h, dp, -1))
                go(h, dp, 0, q, -1, (h, dp, 1))
            elif dq == -1 and dp in (0, 2):
                go(h, dp, dq, q, 1, (h, dp, 2))
            elif dq == 1 and dp in (-1, 1):
                go(h, dp, dq, q, -1, (h, dp, 2))
        for h in range(2):
            multiply(h, dp, dq)

    own = pl.multiple_of(net.c * half, half)
    other = pl.multiple_of((1 - net.c) * half, half)

    def slab(d):
        return lax.rem(net.z + d + PZ, PZ)

    slabs = [4, 3, -3, 2, -2, 1, -1, 0]
    pairs = {}
    for d in slabs:
        pairs[d] = start(net.copy(part.at[slab(d), pl.ds(other, half), :], pair.at[slab(d)], dc=1))
    sub = half // 2

    def rows(u):
        return pl.ds(pl.multiple_of(own + u * sub, sub), sub)

    def merge(d):
        pairs[d].wait_recv()
        part[slab(d), pl.ds(own, half), :] += pair[slab(d)]

    longest = {(0, 1): 4, (0, -1): 3, (1, 1): 3, (1, -1): 4}
    hops = {}

    def hop(u, sign, dist):
        n = len(hops)
        hops[u, sign, dist] = start(net.copy(part.at[slab(sign * dist), rows(u), :], chain.at[n], dz=sign)), n

    def landed(u, sign, dist):
        copy, n = hops[u, sign, dist + 1]
        copy.wait_recv()
        part[slab(sign * dist), rows(u), :] += chain[n]

    merge(4)
    hop(0, 1, 4)
    hop(1, -1, 4)
    merge(3)
    hop(1, 1, 3)
    merge(-3)
    hop(0, -1, 3)
    landed(0, 1, 3)
    hop(0, 1, 3)
    landed(1, -1, 3)
    hop(1, -1, 3)
    merge(2)
    merge(-2)
    for dist in (2, 1):
        for u, sign in ((1, 1), (0, -1), (0, 1), (1, -1)):
            landed(u, sign, dist)
            hop(u, sign, dist)
        if dist == 2:
            merge(1)
            merge(-1)
    merge(0)
    for u, sign in ((1, 1), (0, -1), (0, 1), (1, -1)):
        landed(u, sign, 0)

    def place(u, d, core):
        return out.at[core * 2 + u, pl.ds(pl.multiple_of(slab(d) * 128, 128), 128), :]

    ring = {}

    def send(u, sign, dist):
        where = place(u, -sign * dist, net.c)
        ring[u, sign, dist + 1] = start(net.copy(where, where, dz=sign))

    shared = []

    def share(u, d):
        where = place(u, d, net.c)
        shared.append(start(net.copy(where, where, dc=1)))

    for u in range(2):
        out[net.c * 2 + u, pl.ds(pl.multiple_of(net.z * 128, 128), 128), :] = part[net.z, rows(u), :].T.astype(BF16)
        send(u, 1, 0)
        send(u, -1, 0)
    for u in range(2):
        share(u, 0)
    for dist in range(1, 5):
        for u, sign in ((0, 1), (1, -1), (1, 1), (0, -1)):
            if dist > longest[u, sign]:
                continue
            ring[u, sign, dist].wait_recv()
            if dist < longest[u, sign]:
                send(u, sign, dist)
            share(u, -sign * dist)
    for copy in shared:
        copy.wait_recv()
    for copy in started:
        copy.wait_send()


def column_image(slots, tiles, sketch):
    return pl.pallas_call(
        column_kernel,
        name="column_image",
        out_shape=jax.ShapeDtypeStruct((4, 1024, 128), BF16),
        in_specs=[pl.BlockSpec(memory_space=pltpu.SMEM), pl.BlockSpec(memory_space=pl.ANY), pl.BlockSpec(memory_space=pltpu.VMEM)],
        out_specs=pl.BlockSpec(memory_space=pltpu.VMEM),
        scratch_shapes=[
            pltpu.VMEM((32, EDGE, EDGE), BF16),
            pltpu.VMEM((RB, EDGE, CB * EDGE), BF16),
            pltpu.VMEM((RB, K, EDGE), BF16),
            pltpu.VMEM((8, K, 128), F32),
            pltpu.VMEM((8, EDGE, 128), F32),
            pltpu.VMEM((14, 128, 128), F32),
            pltpu.SemaphoreType.DMA,
            pltpu.SemaphoreType.DMA((100,)),
            pltpu.SemaphoreType.DMA((100,)),
        ],
        compiler_params=pltpu.CompilerParams(collective_id=0, has_side_effects=True, vmem_limit_bytes=56 << 20),
    )(slots, tiles, sketch)


def slot_table(tile_rows, tile_cols, counts):
    slots = jnp.arange(tile_rows.shape[0], dtype=jnp.int32)
    spot = tile_rows * CB + tile_cols
    hit = (spot[None, :] == jnp.arange(RB * CB)[:, None]) & (slots < counts)[None, :]
    return jnp.max(jnp.where(hit, slots[None, :], -1), axis=1)


HIGH = lax.Precision.HIGHEST


def reach():
    steps = [dict(dc=1)]
    steps += [dict(dx=d) for d in (1, -1, 2)]
    steps += [dict(dy=d) for d in (1, -1, 2)]
    steps += [dict(dz=d) for d in (1, -1, 2, -2, 3, -3, 4)]
    return steps


PANELS = [(i, j) for j in range(4) for i in range(j + 1)]
GROWS = 1280


def image_kernel(slot_ref, tiles_hbm, ci, image, gram, tiles, dense, acc, far, sum2, in1, in2, gbuf, gx, gy, gz, gpair, dma_sem, send_sems, recv_sems):
    net = Net(send_sems, recv_sems)
    load = pltpu.make_async_copy(tiles_hbm, tiles, dma_sem)
    load.start()
    net.greet(reach())
    load.wait()
    build_dense(slot_ref, tiles, dense)
    started = []

    def start(copy):
        copy.start()
        started.append(copy)
        return copy

    def begin(copy):
        copy.start()
        return copy

    axes = [("dx", "dy"), ("dy", "dx")]

    def block_of(h, dp, dq):
        dx, dy = (dp, dq) if h == 0 else (dq, dp)
        return lax.rem(net.y + dy + PY, PY) * PX + lax.rem(net.x + dx + PX, PX)

    def product(h, dp, dq):
        left = dense[block_of(h, dp, dq)]
        right = jnp.concatenate([ci[2 * h], ci[2 * h + 1]], axis=1)
        return jnp.dot(left, right, preferred_element_type=F32)

    QS = (2, 1, -1, 0)
    moves = {}

    def send1(h, dp, dq, sign):
        n = len(moves)
        moves[h, dp, dq] = start(net.copy(far.at[n], in1.at[n], **{axes[h][0]: sign})), n

    def via(dq):
        return 1 if dq in (0, 2) else -1

    def fill(h, dp, dq, value):
        far[len(moves)] = value.astype(BF16)

    for dq in QS:
        for h in range(2):
            fill(h, 2, dq, product(h, 2, dq))
            send1(h, 2, dq, via(dq))
    for dq in QS:
        for h in range(2):
            s = -via(dq)
            fill(h, s, dq, product(h, s, dq))
            send1(h, s, dq, s)
    for dq in QS:
        for h in range(2):
            s = via(dq)
            value = product(h, s, dq)
            copy, n = moves[h, 2, dq]
            copy.wait_recv()
            fill(h, s, dq, value + in1[n].astype(F32))
            send1(h, s, dq, s)
    moves2 = {}
    rows_half = EDGE // 2

    def send2(h, dq, piece, sign):
        n = len(moves2)
        part = pl.ds(piece * rows_half, rows_half)
        moves2[h, dq, piece] = start(net.copy(sum2.at[h, dq % 4, part, :], in2.at[n], **{axes[h][1]: sign})), n

    for dq in QS:
        for h in range(2):
            value = product(h, 0, dq)
            for s in (-via(dq), via(dq)):
                copy, n = moves[h, s, dq]
                copy.wait_recv()
                value = value + in1[n].astype(F32)
            sum2[h, dq % 4] = value
            if dq == 2:
                send2(h, 2, 0, 1)
                send2(h, 2, 1, -1)
            elif dq != 0:
                near = 0 if dq == -1 else 1
                send2(h, dq, near, dq)
    for dq in (1, -1):
        for h in range(2):
            through = 0 if dq == 1 else 1
            copy, n = moves2[h, 2, through]
            copy.wait_recv()
            sum2[h, dq % 4, through * rows_half:(through + 1) * rows_half, :] += in2[n]
            send2(h, dq, through, dq)
    for h in range(2):
        for piece in range(2):
            value = sum2[h, 0, piece * rows_half:(piece + 1) * rows_half, :]
            for dq in (1, -1):
                copy, n = moves2[h, dq, piece]
                copy.wait_recv()
                value = value + in2[n]
            image[piece * rows_half:(piece + 1) * rows_half, h * EDGE:(h + 1) * EDGE] = value

    scale = 1.0 / (lax.axis_size("row") * lax.axis_size("blk") * EDGE)
    for n, (i, j) in enumerate(PANELS):
        gbuf[n * 128:(n + 1) * 128, :] = lax.dot_general(
            image[:, i * 128:(i + 1) * 128], image[:, j * 128:(j + 1) * 128], (((0,), (0,)), ((), ())),
            precision=HIGH, preferred_element_type=F32) * scale
    base = pl.multiple_of(net.c * 640, 8)
    pair = start(net.copy(gbuf.at[pl.ds(pl.multiple_of((1 - net.c) * 640, 8), 640), :], gpair, dc=1))
    pair.wait_recv()
    gbuf[pl.ds(base, 640), :] += gpair[...]

    def quarter(at, pos, d, size):
        return pl.ds(pl.multiple_of(at + lax.rem(pos + d + 4, 4) * size, 8), size)

    def spread(axis, pos, at, size, land):
        copies = [begin(net.copy(gbuf.at[quarter(at, pos, d, size), :], land.at[n], **{axis: d})) for n, d in enumerate((2, 1, -1))]
        value = gbuf[quarter(at, pos, 0, size), :]
        for n, copy in enumerate(copies):
            copy.wait_recv()
            value = value + land[n]
        for copy in copies:
            copy.wait_send()
        gbuf[quarter(at, pos, 0, size), :] = value
        return pl.multiple_of(at + pos * size, 8)

    base_x = spread("dx", net.x, base, 160, gx)
    base_y = spread("dy", net.y, base_x, 40, gy)
    copies = [begin(net.copy(gbuf.at[pl.ds(base_y, 40), :], gz.at[n], dz=d)) for n, d in enumerate((4, 3, -3, 2, -2, 1, -1))]
    for copy in copies:
        copy.wait_recv()
    for copy in copies:
        copy.wait_send()
    value = None
    gz[7] = gbuf[pl.ds(base_y, 40), :]
    offsets = (4, 3, -3, 2, -2, 1, -1, 0)
    for place in range(PZ):
        d = lax.rem(net.z - place + PZ, PZ)
        at = 0
        for n, o in enumerate(offsets):
            at = at + jnp.where(d == o % PZ, n, 0)
        term = gz[at]
        value = term if value is None else value + term
    gram[pl.ds(base_y, 40), :] = value

    def collect(axis, at, size):
        where = gram.at[pl.ds(at, size), :]
        copies = [start(net.copy(where, where, **{axis: d})) for d in ((2, 1, -1) if axis != "dc" else (1,))]
        for copy in copies:
            copy.wait_recv()

    collect("dy", base_y, 40)
    collect("dx", base_x, 160)
    collect("dc", base, 640)
    for copy in started:
        copy.wait_send()


def image_and_gram(slots, tiles, ci):
    vmem = pl.BlockSpec(memory_space=pltpu.VMEM)
    return pl.pallas_call(
        image_kernel,
        name="image_and_gram",
        out_shape=[jax.ShapeDtypeStruct((EDGE, K), F32), jax.ShapeDtypeStruct((GROWS, 128), F32)],
        in_specs=[pl.BlockSpec(memory_space=pltpu.SMEM), pl.BlockSpec(memory_space=pl.ANY), vmem],
        out_specs=[vmem, vmem],
        scratch_shapes=[
            pltpu.VMEM((32, EDGE, EDGE), BF16),
            pltpu.VMEM((RB, EDGE, CB * EDGE), BF16),
            pltpu.VMEM((8, 128), F32),
            pltpu.VMEM((24, EDGE, EDGE), BF16),
            pltpu.VMEM((2, 4, EDGE, EDGE), F32),
            pltpu.VMEM((24, EDGE, EDGE), BF16),
            pltpu.VMEM((12, EDGE // 2, EDGE), F32),
            pltpu.VMEM((GROWS, 128), F32),
            pltpu.VMEM((3, 160, 128), F32),
            pltpu.VMEM((3, 40, 128), F32),
            pltpu.VMEM((8, 40, 128), F32),
            pltpu.VMEM((640, 128), F32),
            pltpu.SemaphoreType.DMA,
            pltpu.SemaphoreType.DMA((64,)),
            pltpu.SemaphoreType.DMA((64,)),
        ],
        compiler_params=pltpu.CompilerParams(collective_id=1, has_side_effects=True, vmem_limit_bytes=56 << 20),
    )(slots, tiles, ci)


def lane(x, j):
    return jnp.take_along_axis(x, jnp.full(x.shape, j, jnp.int32), axis=1)


def sub(x, i):
    return jnp.broadcast_to(x[i:i + 1, :], x.shape)


def factor_block(S, E):
    rid = lax.broadcasted_iota(jnp.int32, (8, 128), 0)
    lid = lax.broadcasted_iota(jnp.int32, (8, 128), 1)
    E = [(lid == rid + 8 * i).astype(F32) for i in range(16)]
    S = list(S)
    for g in range(16):
        cols = [lane(S[g], 8 * g + k) for k in range(8)]
        a = {(i, k): sub(cols[k], i) for k in range(8) for i in range(k, 8)}
        r, l, m = [None] * 8, {}, {}
        for k in range(8):
            r[k] = lax.rsqrt(a[k, k])
            for i in range(k + 1, 8):
                l[i, k] = a[i, k] * r[k]
            for i in range(k + 1, 8):
                for n in range(k + 1, i + 1):
                    a[i, n] = a[i, n] - l[i, k] * l[n, k]
        for j in range(8):
            m[j, j] = r[j]
            for i in range(j + 1, 8):
                t = l[i, j] * m[j, j]
                for k in range(j + 1, i):
                    t = t + l[i, k] * m[k, j]
                m[i, j] = -(t * r[i])
        u = e = None
        for k in range(8):
            c = jnp.zeros((8, 128), F32)
            for i in range(k, 8):
                c = jnp.where(rid == i, m[i, k], c)
            tu, te = c * sub(S[g], k), c * sub(E[g], k)
            u, e = (tu, te) if u is None else (u + tu, e + te)
        S[g], E[g] = u, e
        if g < 15:
            us, es = [sub(u, k) for k in range(8)], [sub(e, k) for k in range(8)]
            turned = u.T
            for i in range(g + 1, 16):
                c = turned[8 * i:8 * i + 8, :]
                for k in range(8):
                    ck = jnp.broadcast_to(c[:, k:k + 1], (8, 128))
                    S[i] = S[i] - ck * us[k]
                    E[i] = E[i] - ck * es[k]
    S = [jnp.where(lid >= rid + 8 * i, s, 0.0) for i, s in enumerate(S)]
    return S, E


def dot(a, b, dims=((1,), (0,))):
    return lax.dot_general(a, b, (dims, ((), ())), precision=HIGH, preferred_element_type=F32)


def basis_kernel(gram, image, basis, factor, S, inv):
    def panel(i, j):
        return slice(j * 128, (j + 1) * 128), slice(i * 128, (i + 1) * 128)

    index = {p: n for n, p in enumerate(PANELS)}
    for (i, j), n in index.items():
        S[n] = gram[n * 128:(n + 1) * 128, :]
    span = lambda b: slice(b * 128, (b + 1) * 128)
    for b in range(4):
        for i in range(b):
            factor[span(b), span(i)] = jnp.zeros((128, 128), F32)

    for b in range(4):
        d = index[b, b]
        if b:
            for k in range(b):
                u = factor[span(k), span(b)]
                for j in range(b, 4):
                    pass
        rows = [S[d, 8 * g:8 * g + 8, :] for g in range(16)]
        rows, e = factor_block(rows, None)
        for g in range(16):
            factor[b * 128 + 8 * g:b * 128 + 8 * g + 8, span(b)] = rows[g]
            inv[8 * g:8 * g + 8, :] = e[g]
        for j in range(b + 1, 4):
            factor[span(b), span(j)] = dot(inv[...], S[index[b, j]])
        for i in range(b + 1, 4):
            for j in range(i, 4):
                S[index[i, j]] -= dot(factor[span(b), span(i)], factor[span(b), span(j)], ((0,), (0,)))
        value = image[:, span(b)]
        for k in range(b):
            value = value - dot(basis[:, span(k)], factor[span(k), span(b)])
        basis[:, span(b)] = dot(value, inv[...], ((1,), (1,)))


def orthonormalize(gram, image):
    vmem = pl.BlockSpec(memory_space=pltpu.VMEM)
    return pl.pallas_call(
        basis_kernel,
        name="orthonormalize",
        out_shape=[jax.ShapeDtypeStruct((EDGE, K), F32), jax.ShapeDtypeStruct((K, K), F32)],
        in_specs=[vmem, vmem],
        out_specs=[vmem, vmem],
        scratch_shapes=[pltpu.VMEM((10, 128, 128), F32), pltpu.VMEM((128, 128), F32)],
        compiler_params=pltpu.CompilerParams(vmem_limit_bytes=32 << 20),
    )(gram, image)


def local(tiles, tile_rows, tile_cols, counts, sketch):
    blocks = tiles[0, 0]
    slots = slot_table(tile_rows[0, 0], tile_cols[0, 0], counts[0, 0])
    ci = column_image(slots, blocks, sketch)
    image, gram = image_and_gram(slots, blocks, ci)
    return orthonormalize(gram, image)


def solution(mesh):
    in_specs = (
        P("row", "blk", None, None, None),
        P("row", "blk", None),
        P("row", "blk", None),
        P("row", "blk"),
        P(("row", "blk"), None),
    )
    out_specs = (P(("row", "blk"), None), P())
    return jax.shard_map(local, mesh=mesh, in_specs=in_specs, out_specs=out_specs, check_vma=False)
```

time: 661 us -> 164 us (0.25); the launches traced: 652 us -> 164 us
  waiting for transfers between devices: 372 us -> 0 us
  Pallas kernels: 0 us -> 159 us
  other arithmetic: 122 us -> 1.29 us
  blocking collectives: 58.2 us -> 0 us
  local copies, waits for them, and re-layouts: 44 us -> 2.12 us
  matrix products: 37.7 us -> 0 us
  between operations: 17.6 us -> 1.31 us
    psum x1 -> x0, waiting for transfers between devices: 258 us -> none  [local(): gram = lax.psum(local_gram, ('row', 'blk'))]
    pallas_call x0 -> x3, Pallas kernels: none -> 159 us  [the longest x1 69.6 us: column_image(): pl.pallas_call(column_kernel, name='column_image', out_shape=jax.ShapeDty...]
    another operation x17 -> x0, other arithmetic: 118 us -> none  [the longest x14 78.9 us: local(): lower = jnp.linalg.cholesky(gram)]
    reduce_scatter x1 -> x0, waiting for transfers between devices: 88.9 us -> none  [local(): lax.psum_scatter(jnp.dot(dense, column_image, preferred_element_type=jnp....]
    psum x1 -> x0, blocking collectives: 58.2 us -> none  [local(): column_image = lax.psum(partial_value, 'row').astype(jnp.bfloat16)]
    dot_general x4 -> x0, matrix products: 30.1 us -> none  [the longest x1 10.4 us: local(): jnp.dot(dense, column_image, preferred_element_type=jnp.float32)]
    all_gather x1 -> x0, waiting for transfers between devices: 24.2 us -> none  [local(): gathered = lax.all_gather(sketch, 'blk', axis=0, tiled=True)]
    convert_element_type x1 -> x0, local copies, waits for them, and re-layouts: 16.1 us -> none  [local(): dense = dense.astype(jnp.bfloat16).reshape(RB * edge, CB * edge)]
  transfers between devices with their start and end apart: 3 -> 0, of which waited for: 3 -> 0; matrix products, arithmetic and copies ran while one was open for 6% -> 0% of each run, Pallas kernels for 0% -> 0%
where the time goes in v1:
time: 164 us
  Pallas kernels  159 us (97%)
  local copies, waits for them, and re-layouts  2.12 us (1%)
    pallas_call x1, Pallas kernels, column_image(): pl.pallas_call(column_kernel, name='column_image', out_shape=jax.ShapeDty...  69.6 us
    pallas_call x1, Pallas kernels, image_and_gram(): pl.pallas_call(image_kernel, name='image_and_gram', out_shape=[jax.ShapeD...  64.6 us
    pallas_call x1, Pallas kernels, orthonormalize(): pl.pallas_call(basis_kernel, name='orthonormalize', out_shape=[jax.ShapeD...  24.8 us

profile of v1, /device:TPU:1, one launch (start us, length us, event | category | flops | bytes accessed | tf_op | source)
XLA Modules:
  0.0 163.8 jit_solution(3756820654335113923)
XLA Ops:
  1.3 0.7 add_bitcast_fusion
  2.0 0.6 select_reduce_fusion.slot_ref
  2.6 69.6 %column_image.1.ci = bf16[4,1024,128]{2,1,0:T(8,128)(2,1)} custom-call(s32[64]{0:T(128)} %select_reduce_fusion.slot_ref, bf16[32,256,256]{2,1,0:T(8,128)(2,1)} %bitcast.5, bf16[256,512]{1,0:T(8,128)(2,1)} %sketch_ref.1), custom_call_target="tpu_custom_call" | custom-call | tf_op jit(solution)/shard_map/column_image/pallas_call | solution.py:237
  72.2 64.6 %image_and_gram.1 = (f32[256,512]{1,0:T(8,128)}, f32[1280,128]{1,0:T(8,128)}) custom-call(s32[64]{0:T(128)} %select_reduce_fusion.slot_ref, bf16[32,256,256]{2,1,0:T(8,128)(2,1)} %bitcast.6, bf16[4,1024,128]{2,1,0:T(8,128)(2,1)} %column_image.1.ci), custom_call_target="tpu_custom_call" | custom-call | tf_op jit(solution)/shard_map/image_and_gram/pallas_call | solution.py:435
  136.9 0.0 copy-start
  136.9 1.1 copy-done
  137.9 0.0 copy-start.1
  137.9 1.0 copy-done.1
  139.0 24.8 %orthonormalize.1 = (f32[256,512]{1,0:T(8,128)}, f32[512,512]{1,0:T(8,128)}) custom-call(f32[1280,128]{1,0:T(8,128)S(1)} %copy-done, f32[256,512]{1,0:T(8,128)S(1)} %copy-done.1), custom_call_target="tpu_custom_call" | custom-call | tf_op jit(solution)/shard_map/orthonormalize/pallas_call | solution.py:555
  (1 shorter events, 0.0 us)
Async XLA Ops:
  136.9 1.1 copy-start
  137.9 1.0 copy-start.1

commit v2 on v0

v2 whole, which is shorter than its diff:
```python
import functools
import jax
import jax.numpy as jnp
from jax import lax
from jax.experimental import pallas as pl
from jax.experimental.pallas import tpu as pltpu
from jax.sharding import PartitionSpec as P

F32 = jnp.float32
BF16 = jnp.bfloat16
MESH = pl.DeviceIdType.MESH
EDGE = 256
RB = 16
CB = 4
K = 512
PX, PY, PZ = 4, 4, 8


def where_am_i():
    row = lax.axis_index("row")
    blk = lax.axis_index("blk")
    return row // 2, row % 2, blk // PX, blk % PX


class Net:
    def __init__(self, send_sems, recv_sems):
        self.send_sems, self.recv_sems = send_sems, recv_sems
        self.used = 0
        self.z, self.c, self.y, self.x = where_am_i()

    def device(self, dz=0, dc=0, dy=0, dx=0):
        z = lax.rem(self.z + dz + PZ, PZ)
        c = 1 - self.c if dc else self.c
        y = lax.rem(self.y + dy + PY, PY)
        x = lax.rem(self.x + dx + PX, PX)
        return {"row": z * 2 + c, "blk": y * PX + x}

    def greet(self, steps):
        barrier = pltpu.get_barrier_semaphore()
        for step in steps:
            pl.semaphore_signal(barrier, inc=1, device_id=self.device(**step), device_id_type=MESH)
        pl.semaphore_wait(barrier, len(steps))

    def copy(self, src, dst, **step):
        slot = self.used
        self.used += 1
        return pltpu.make_async_remote_copy(
            src_ref=src, dst_ref=dst, send_sem=self.send_sems.at[slot], recv_sem=self.recv_sems.at[slot],
            device_id=self.device(**step), device_id_type=MESH)


NEIGHBOURS = [dict(dx=1), dict(dx=-1), dict(dy=1), dict(dy=-1), dict(dz=1), dict(dz=-1), dict(dc=1)]


def build_dense(slot_ref, tiles, dense):
    @pl.loop(0, RB)
    def _(i):
        for c in range(CB):
            slot = slot_ref[i * CB + c]
            keep = jnp.where(slot >= 0, 1.0, 0.0).astype(BF16)
            dense[i, :, c * EDGE:(c + 1) * EDGE] = tiles[jnp.maximum(slot, 0)] * keep


def slot_table(tile_rows, tile_cols, counts):
    slots = jnp.arange(tile_rows.shape[0], dtype=jnp.int32)
    spot = tile_rows * CB + tile_cols
    hit = (spot[None, :] == jnp.arange(RB * CB)[:, None]) & (slots < counts)[None, :]
    return jnp.max(jnp.where(hit, slots[None, :], -1), axis=1)


HIGH = lax.Precision.HIGHEST


def reach():
    steps = [dict(dc=1)]
    steps += [dict(dx=d) for d in (1, -1, 2)]
    steps += [dict(dy=d) for d in (1, -1, 2)]
    steps += [dict(dz=d) for d in (1, -1, 2, -2, 3, -3, 4)]
    return steps


PANELS = [(i, j) for j in range(4) for i in range(j + 1)]

GR = (512, 1024)


def lane(x, j):
    return jnp.take_along_axis(x, jnp.full(x.shape, j, jnp.int32), axis=1)


def sub(x, i):
    return jnp.broadcast_to(x[i:i + 1, :], x.shape)


def factor_block(S, E):
    rid = lax.broadcasted_iota(jnp.int32, (8, 128), 0)
    lid = lax.broadcasted_iota(jnp.int32, (8, 128), 1)
    E[:] = [(lid == rid + 8 * i).astype(F32) for i in range(16)]
    for g in range(16):
        cols = [lane(S[g], 8 * g + k) for k in range(8)]
        a = {(i, k): sub(cols[k], i) for k in range(8) for i in range(k, 8)}
        r, l, m = [None] * 8, {}, {}
        for k in range(8):
            r[k] = lax.rsqrt(a[k, k])
            for i in range(k + 1, 8):
                l[i, k] = a[i, k] * r[k]
            for i in range(k + 1, 8):
                for n in range(k + 1, i + 1):
                    a[i, n] = a[i, n] - l[i, k] * l[n, k]
        for j in range(8):
            m[j, j] = r[j]
            for i in range(j + 1, 8):
                t = l[i, j] * m[j, j]
                for k in range(j + 1, i):
                    t = t + l[i, k] * m[k, j]
                m[i, j] = -(t * r[i])
        u = e = None
        for k in range(8):
            c = jnp.zeros((8, 128), F32)
            for i in range(k, 8):
                c = jnp.where(rid == i, m[i, k], c)
            tu, te = c * sub(S[g], k), c * sub(E[g], k)
            u, e = (tu, te) if u is None else (u + tu, e + te)
        S[g], E[g] = u, e
        if g < 15:
            us, es = [sub(u, k) for k in range(8)], [sub(e, k) for k in range(8)]
            turned = u.T
            for i in range(g + 1, 16):
                c = turned[8 * i:8 * i + 8, :]
                for k in range(8):
                    ck = jnp.broadcast_to(c[:, k:k + 1], (8, 128))
                    S[i] = S[i] - ck * us[k]
                    E[i] = E[i] - ck * es[k]
            yield CHOL
    S[:] = [jnp.where(lid >= rid + 8 * i, s, 0.0) for i, s in enumerate(S)]


def dot(a, b, dims=((1,), (0,))):
    return lax.dot_general(a, b, (dims, ((), ())), precision=HIGH, preferred_element_type=F32)


def weave(*works):
    queue = [[begin, n, work] for n, (begin, work) in enumerate(works)]
    while queue:
        entry = min(queue)
        try:
            entry[0] += next(entry[2])
        except StopIteration:
            queue.remove(entry)


def power_kernel(slot_ref, tiles_hbm, sketch_ref, basis, factor, image, gram0, gram1, S, inv, tiles, dense, gath, part, pair, chain, ci, acc, far, in1, sum2, in2,
                 gbuf0, gbuf1, gpair, g1, g2, gstage, gz, dma_sem, send_sems, recv_sems):
    net = Net(send_sems, recv_sems)
    load = pltpu.make_async_copy(tiles_hbm, tiles, dma_sem)
    load.start()
    mine = net.y * PX + net.x
    gath[mine] = sketch_ref[...].astype(F32).T.astype(BF16)
    net.greet(reach())
    started = []
    axes = [("dx", "dy"), ("dy", "dx")]

    def start(copy):
        copy.start()
        started.append(copy)
        return copy

    def begin(copy):
        copy.start()
        return copy

    def block_of(h, dp, dq):
        dx, dy = (dp, dq) if h == 0 else (dq, dp)
        return lax.rem(net.y + dy + PY, PY) * PX + lax.rem(net.x + dx + PX, PX)

    def slab(d):
        return lax.rem(net.z + d + PZ, PZ)

    def gather(t):
        base = 256 * t
        arrive = {}
        got = set()

        def go(h, dp, dq, axis, sign, key):
            where = gath.at[block_of(h, dp, dq), pl.ds(base + h * 128, 128), :]
            arrive[key] = net.used
            start(net.copy(where, where, **{axis: sign}))

        def received(h, dp, dq):
            where = gath.at[block_of(h, dp, dq), pl.ds(base + h * 128, 128), :]
            n = arrive[h, dp, dq]
            pltpu.make_async_remote_copy(
                src_ref=where, dst_ref=where, send_sem=send_sems.at[n], recv_sem=recv_sems.at[n],
                device_id=net.device(dx=1), device_id_type=MESH).wait_recv()

        def multiply(dx, dy):
            i = block_of(0, dx, dy)
            block = gath[i, base:base + 256, :]
            for c in range(CB):
                prod = jnp.dot(block, dense[i, :, c * EDGE:(c + 1) * EDGE], preferred_element_type=F32)
                for s in range(2):
                    piece = prod[:, s * 128:(s + 1) * 128]
                    if (dx, dy) == (0, 0):
                        part[2 * c + s, base:base + 256, :] = piece
                    else:
                        part[2 * c + s, base:base + 256, :] += piece

        for h in range(2):
            p, q = axes[h]
            go(h, 0, 0, p, 1, (h, -1, 0))
            go(h, 0, 0, p, -1, (h, 1, 0))
        for h in range(2):
            p, q = axes[h]
            go(h, 0, 0, q, 1, (h, 0, -1))
            go(h, 0, 0, q, -1, (h, 0, 1))
        if t == 0:
            load.wait()
            build_dense(slot_ref, tiles, dense)
        yield GATHER[t][0]
        multiply(0, 0)
        order = [(-1, 0), (1, 0), (0, -1), (0, 1), (2, 0), (-1, -1), (-1, 1), (0, 2), (1, -1), (1, 1), (-1, 2), (2, -1), (2, 1), (1, 2), (2, 2)]
        for dp, dq in order:
            for h in range(2):
                p, q = axes[h]
                received(h, dp, dq)
                if dq == 0:
                    if dp == -1:
                        go(h, dp, 0, p, 1, (h, 2, 0))
                    go(h, dp, 0, q, 1, (h, dp, -1))
                    go(h, dp, 0, q, -1, (h, dp, 1))
                elif dq == -1 and dp in (0, 2):
                    go(h, dp, dq, q, 1, (h, dp, 2))
                elif dq == 1 and dp in (-1, 1):
                    go(h, dp, dq, q, -1, (h, dp, 2))
            got.add((dp, dq))
            if (dq, dp) in got:
                for dx, dy in {(dp, dq): 0, (dq, dp): 0}:
                    multiply(dx, dy)
            yield GATHER[t][1]

    def columns(t):
        base = 256 * t
        own = pl.multiple_of(base + net.c * 128, 128)
        other = pl.multiple_of(base + (1 - net.c) * 128, 128)
        pairs, legs, shared = {}, {}, []

        def merge(d):
            pairs[d].wait_recv()
            part[slab(d), pl.ds(own, 128), :] += pair[t, slab(d)]

        def leg(name, d, u, slot, dz):
            src = part.at[slab(d), pl.ds(own, 128) if u is None else pl.ds(pl.multiple_of(own + u * 64, 64), 64), :]
            dst = chain.at[t, slot] if u is None else chain.at[t, slot, pl.ds(0, 64), :]
            legs[name] = start(net.copy(src, dst, dz=dz))

        for d in (4, 3, -3, 1, -1, 2, -2, 0):
            pairs[d] = start(net.copy(part.at[slab(d), pl.ds(other, 128), :], pair.at[t, slab(d)], dc=1))
        yield ZPAIR
        merge(4)
        leg((4, 1), 4, 0, 0, 2)
        leg((4, -1), 4, 1, 1, -2)
        merge(3)
        leg((3, 1), 3, None, 2, 1)
        merge(-3)
        leg((3, -1), -3, None, 3, -1)
        merge(1)
        leg((1, 1), 1, None, 4, 1)
        merge(-1)
        leg((1, -1), -1, None, 5, -1)
        merge(2)
        merge(-2)
        yield ZFAR
        for n, sign in enumerate((1, -1)):
            legs[3, sign].wait_recv()
            part[slab(2 * sign), pl.ds(own, 128), :] += chain[t, 2 + n]
            legs[4, sign].wait_recv()
            part[slab(2 * sign), pl.ds(pl.multiple_of(own + n * 64, 64), 64), :] += chain[t, n, 0:64, :]
            leg((2, sign), 2 * sign, None, 6 + n, 2 * sign)
        merge(0)
        yield ZNEAR
        value = part[net.z, pl.ds(own, 128), :]
        for n, sign in enumerate((1, -1)):
            legs[1, sign].wait_recv()
            value = value + chain[t, 4 + n]
        yield ZLAST
        for n, sign in enumerate((1, -1)):
            legs[2, sign].wait_recv()
            value = value + chain[t, 6 + n]

        def place(d, u=None):
            at = slab(d) * 128 + (0 if u is None else u * 64)
            return ci.at[2 * t + net.c, pl.ds(pl.multiple_of(at, 64), 128 if u is None else 64), :]

        def send(d, dz, u=None):
            return start(net.copy(place(d, u), place(d, u), dz=dz))

        def share(d, u=None):
            shared.append(start(net.copy(place(d, u), place(d, u), dc=1)))

        ci[2 * t + net.c, pl.ds(pl.multiple_of(net.z * 128, 128), 128), :] = value.T.astype(BF16)
        two = {sign: send(0, 2 * sign) for sign in (1, -1)}
        one = {sign: send(0, sign) for sign in (1, -1)}
        share(0)
        yield ZRING
        three, four = {}, {}
        for n, sign in enumerate((1, -1)):
            two[sign].wait_recv()
            four[sign] = send(-2 * sign, 2 * sign, n)
            three[sign] = send(-2 * sign, sign)
            share(-2 * sign)
        for sign in (1, -1):
            one[sign].wait_recv()
            share(-sign)
        yield ZRING
        for sign in (1, -1):
            three[sign].wait_recv()
            share(-3 * sign)
        for n, sign in enumerate((1, -1)):
            four[sign].wait_recv()
            share(4, n)
        yield ZSHARE
        for copy in shared:
            copy.wait_recv()

    def rows_out(t):
        moves, moves2, made = {}, {}, set()
        QS = (2, 1, -1, 0)

        def product(h, dp, dq):
            spot = (dp, dq) if h == 0 else (dq, dp)
            i = block_of(h, dp, dq)
            if spot not in made:
                made.add(spot)
                right = jnp.concatenate([ci[2 * t], ci[2 * t + 1]], axis=1)
                acc[t, i] = jnp.dot(dense[i], right, preferred_element_type=F32)
            return acc[t, i, :, h * 128:(h + 1) * 128]

        def send1(h, dp, dq, sign, value):
            n = len(moves)
            far[t, n] = value.astype(BF16)
            moves[h, dp, dq] = start(net.copy(far.at[t, n], in1.at[t, n], **{axes[h][0]: sign})), n

        def via(dq):
            return 1 if dq in (0, 2) else -1

        def send2(h, dq, piece, sign):
            n = len(moves2)
            moves2[h, dq, piece] = start(net.copy(sum2.at[t, h, dq % 4, pl.ds(piece * 128, 128), :], in2.at[t, n], **{axes[h][1]: sign})), n

        for dq in QS:
            for h in range(2):
                send1(h, 2, dq, via(dq), product(h, 2, dq))
        for dq in QS:
            for h in range(2):
                s = -via(dq)
                send1(h, s, dq, s, product(h, s, dq))
        for dq in QS:
            for h in range(2):
                product(h, via(dq), dq)
                product(h, 0, dq)
            yield RS1[QS.index(dq)]
            for h in range(2):
                s = via(dq)
                copy, n = moves[h, 2, dq]
                copy.wait_recv()
                send1(h, s, dq, s, product(h, s, dq) + in1[t, n].astype(F32))
        for dq in QS:
            yield RS2[QS.index(dq)]
            for h in range(2):
                value = product(h, 0, dq)
                for s in (-via(dq), via(dq)):
                    copy, n = moves[h, s, dq]
                    copy.wait_recv()
                    value = value + in1[t, n].astype(F32)
                sum2[t, h, dq % 4] = value
                if dq == 2:
                    send2(h, 2, 0, 1)
                    send2(h, 2, 1, -1)
                elif dq != 0:
                    send2(h, dq, 0 if dq == -1 else 1, dq)
        for dq in (1, -1):
            yield RS3[dq == -1]
            for h in range(2):
                through = 0 if dq == 1 else 1
                copy, n = moves2[h, 2, through]
                copy.wait_recv()
                sum2[t, h, dq % 4, through * 128:(through + 1) * 128, :] += in2[t, n]
                send2(h, dq, through, dq)
        yield RS4
        for h in range(2):
            for piece in range(2):
                value = sum2[t, h, 0, piece * 128:(piece + 1) * 128, :]
                for dq in (1, -1):
                    copy, n = moves2[h, dq, piece]
                    copy.wait_recv()
                    value = value + in2[t, n]
                image[piece * 128:(piece + 1) * 128, t * 256 + h * 128:t * 256 + (h + 1) * 128] = value

    def moments(t):
        size = GR[t]
        gbuf, out = (gbuf0, gram0) if t == 0 else (gbuf1, gram1)
        scale = 1.0 / (lax.axis_size("row") * lax.axis_size("blk") * EDGE)
        panels = [p for p in PANELS if p[1] // 2 == t]
        for n, (i, j) in enumerate(panels):
            gbuf[n * 128:(n + 1) * 128, :] = lax.dot_general(
                image[:, i * 128:(i + 1) * 128], image[:, j * 128:(j + 1) * 128], (((0,), (0,)), ((), ())),
                precision=HIGH, preferred_element_type=F32) * scale
        gbuf[size - 128:, :] = jnp.zeros((128, 128), F32)
        half, quarter, first, second = size // 2, size // 4, size // 16, size // 64
        base = pl.multiple_of(net.c * half, 256)
        twin = start(net.copy(gbuf.at[pl.ds(pl.multiple_of((1 - net.c) * half, 256), half), :], gpair.at[pl.ds(t * 256, half), :], dc=1))
        yield GM1
        twin.wait_recv()
        gbuf[pl.ds(base, half), :] += gpair[t * 256:t * 256 + half, :]

        def cut(at, pos, d, step):
            return pl.ds(pl.multiple_of(at + lax.rem(pos + d + 4, 4) * step, 8), step)

        place = (net.x, net.y)
        ats = [base + v * quarter for v in range(2)]
        for level, step in enumerate((first, second)):
            copies = {}
            for d in (2, 1, -1):
                for v in range(2):
                    n = {2: 0, 1: 1, -1: 2}[d]
                    land = g1.at[t, v, n, pl.ds(0, step), :] if level == 0 else g2.at[t, v, n, pl.ds(0, step), :]
                    axis = axes[v][level]
                    copies[v, n] = start(net.copy(gbuf.at[cut(ats[v], place[(v + level) % 2], d, step), :], land, **{axis: d}))
            yield GM2
            for v in range(2):
                here = cut(ats[v], place[(v + level) % 2], 0, step)
                value = gbuf[here, :]
                for n in range(3):
                    copies[v, n].wait_recv()
                    value = value + (g1 if level == 0 else g2)[t, v, n, 0:step, :]
                if level == 0:
                    gbuf[here, :] = value
                else:
                    gstage[t, v * second:(v + 1) * second, :] = value
                ats[v] = pl.multiple_of(ats[v] + place[(v + level) % 2] * step, 8)
        both = 2 * second
        offsets = (4, 3, -3, 2, -2, 1, -1, 0)
        copies = [start(net.copy(gstage.at[t, pl.ds(0, both), :], gz.at[t, n, pl.ds(0, both), :], dz=d)) for n, d in enumerate(offsets[:-1])]
        gz[t, 7, 0:both, :] = gstage[t, 0:both, :]
        yield GM3
        for copy in copies:
            copy.wait_recv()
        value = None
        for spot in range(PZ):
            d = lax.rem(net.z - spot + PZ, PZ)
            at = 0
            for n, o in enumerate(offsets):
                at = at + jnp.where(d == o % PZ, n, 0)
            term = gz[t, at, 0:both, :]
            value = term if value is None else value + term
        for v in range(2):
            out[pl.ds(ats[v], second), :] = value[v * second:(v + 1) * second, :]
        for level, step in ((1, second), (0, first)):
            copies = []
            for v in range(2):
                if level == 0:
                    ats[v] = base + v * quarter + place[v % 2] * first
                where = out.at[pl.ds(pl.multiple_of(ats[v], 8), step), :]
                for d in (2, 1, -1):
                    copies.append(start(net.copy(where, where, **{axes[v][level]: d})))
            yield GM2
            for copy in copies:
                copy.wait_recv()
        where = out.at[pl.ds(base, half), :]
        twin = start(net.copy(where, where, dc=1))
        yield GM1
        twin.wait_recv()

    index = {p: n for n, p in enumerate(PANELS)}

    def span(b):
        return slice(b * 128, (b + 1) * 128)

    def panel(i, j):
        n = index[i, j]
        return gram0[span(n), :] if n < 3 else gram1[span(n - 3), :]

    def reduced(i, j, upto):
        value = panel(i, j)
        for k in range(upto):
            value = value - dot(factor[span(k), span(i)], factor[span(k), span(j)], ((0,), (0,)))
        return value

    def solve(b):
        for i in range(b):
            factor[span(b), span(i)] = jnp.zeros((128, 128), F32)
        if b == 2:
            for j in (2, 3):
                for i in (0, 1):
                    factor[span(i), span(j)] = dot(inv[i], reduced(i, j, i))
        yield CHOL
        S[...] = reduced(b, b, b)
        value = image[:, span(b)]
        for k in range(b):
            value = value - dot(basis[:, span(k)], factor[span(k), span(b)])
        yield CHOL
        rows, e = [S[8 * g:8 * g + 8, :] for g in range(16)], []
        yield from factor_block(rows, e)
        for g in range(16):
            factor[b * 128 + 8 * g:b * 128 + 8 * g + 8, span(b)] = rows[g]
            inv[b, 8 * g:8 * g + 8, :] = e[g]
        yield CHOL
        if b % 2 == 0:
            factor[span(b), span(b + 1)] = dot(inv[b], reduced(b, b + 1, b))
        yield CHOL
        basis[:, span(b)] = dot(value, inv[b], ((1,), (1,)))

    def process(t):
        yield from gather(t)
        yield from columns(t)
        yield from rows_out(t)
        yield from moments(t)

        if t == 0:
            yield from solve(0)
            yield from solve(1)

    weave((0.0, process(0)), (SECOND, process(1)))
    weave((0.0, solve(2)))
    weave((0.0, solve(3)))
    for copy in started:
        copy.wait_send()


SECOND = 15.0
GATHER = ((8.0, 1.0), (5.0, 1.2))
ZPAIR, ZFAR, ZNEAR, ZLAST, ZRING, ZSHARE = 3.0, 4.5, 1.0, 3.0, 3.5, 1.5
RS1, RS2, RS3, RS4 = (4.0, 1.2, 1.2, 1.2), (2.5, 1.2, 1.2, 1.2), (1.5, 0.7), 2.5
GM1, GM2, GM3 = 2.0, 3.0, 6.0
CHOL = 0.45


def power_step(slots, tiles, sketch):
    vmem = pl.BlockSpec(memory_space=pltpu.VMEM)
    return pl.pallas_call(
        power_kernel,
        name="power_step",
        out_shape=[jax.ShapeDtypeStruct((EDGE, K), F32), jax.ShapeDtypeStruct((K, K), F32)],
        in_specs=[pl.BlockSpec(memory_space=pltpu.SMEM), pl.BlockSpec(memory_space=pl.ANY), vmem],
        out_specs=[vmem, vmem],
        scratch_shapes=[
            pltpu.VMEM((EDGE, K), F32),
            pltpu.VMEM((GR[0], 128), F32),
            pltpu.VMEM((GR[1], 128), F32),
            pltpu.VMEM((128, 128), F32),
            pltpu.VMEM((4, 128, 128), F32),
            pltpu.VMEM((32, EDGE, EDGE), BF16),
            pltpu.VMEM((RB, EDGE, CB * EDGE), BF16),
            pltpu.VMEM((RB, K, EDGE), BF16),
            pltpu.VMEM((8, K, 128), F32),
            pltpu.VMEM((2, 8, 128, 128), F32),
            pltpu.VMEM((2, 8, 128, 128), F32),
            pltpu.VMEM((4, 1024, 128), BF16),
            pltpu.VMEM((2, RB, EDGE, EDGE), F32),
            pltpu.VMEM((2, 24, EDGE, 128), BF16),
            pltpu.VMEM((2, 24, EDGE, 128), BF16),
            pltpu.VMEM((2, 2, 4, EDGE, 128), F32),
            pltpu.VMEM((2, 12, 128, 128), F32),
            pltpu.VMEM((GR[0], 128), F32),
            pltpu.VMEM((GR[1], 128), F32),
            pltpu.VMEM((768, 128), F32),
            pltpu.VMEM((2, 2, 3, 64, 128), F32),
            pltpu.VMEM((2, 2, 3, 16, 128), F32),
            pltpu.VMEM((2, 32, 128), F32),
            pltpu.VMEM((2, 8, 32, 128), F32),
            pltpu.SemaphoreType.DMA,
            pltpu.SemaphoreType.DMA((320,)),
            pltpu.SemaphoreType.DMA((320,)),
        ],
        compiler_params=pltpu.CompilerParams(collective_id=0, has_side_effects=True, vmem_limit_bytes=60 << 20),
    )(slots, tiles, sketch)


def local(tiles, tile_rows, tile_cols, counts, sketch):
    blocks = tiles[0, 0]
    slots = slot_table(tile_rows[0, 0], tile_cols[0, 0], counts[0, 0])
    basis, factor = power_step(slots, blocks, sketch)
    return basis, factor


def solution(mesh):
    in_specs = (
        P("row", "blk", None, None, None),
        P("row", "blk", None),
        P("row", "blk", None),
        P("row", "blk"),
        P(("row", "blk"), None),
    )
    out_specs = (P(("row", "blk"), None), P())
    return jax.shard_map(local, mesh=mesh, in_specs=in_specs, out_specs=out_specs, check_vma=False)
```

time: 661 us -> 158 us (0.24); the launches traced: 652 us -> 158 us
  waiting for transfers between devices: 372 us -> 0 us
  Pallas kernels: 0 us -> 151 us
  other arithmetic: 122 us -> 1.29 us
  blocking collectives: 58.2 us -> 0 us
  local copies, waits for them, and re-layouts: 44 us -> 4.13 us
  matrix products: 37.7 us -> 0 us
  between operations: 17.6 us -> 1.29 us
    psum x1 -> x0, waiting for transfers between devices: 258 us -> none  [local(): gram = lax.psum(local_gram, ('row', 'blk'))]
    pallas_call x0 -> x1, Pallas kernels: none -> 151 us  [power_step(): pl.pallas_call(power_kernel, name='power_step', out_shape=[jax.ShapeDtype...]
    another operation x17 -> x0, other arithmetic: 118 us -> none  [the longest x14 78.9 us: local(): lower = jnp.linalg.cholesky(gram)]
    reduce_scatter x1 -> x0, waiting for transfers between devices: 88.9 us -> none  [local(): lax.psum_scatter(jnp.dot(dense, column_image, preferred_element_type=jnp....]
    psum x1 -> x0, blocking collectives: 58.2 us -> none  [local(): column_image = lax.psum(partial_value, 'row').astype(jnp.bfloat16)]
    dot_general x4 -> x0, matrix products: 30.1 us -> none  [the longest x1 10.4 us: local(): jnp.dot(dense, column_image, preferred_element_type=jnp.float32)]
    all_gather x1 -> x0, waiting for transfers between devices: 24.2 us -> none  [local(): gathered = lax.all_gather(sketch, 'blk', axis=0, tiled=True)]
    convert_element_type x1 -> x0, local copies, waits for them, and re-layouts: 16.1 us -> none  [local(): dense = dense.astype(jnp.bfloat16).reshape(RB * edge, CB * edge)]
  transfers between devices with their start and end apart: 3 -> 0, of which waited for: 3 -> 0; matrix products, arithmetic and copies ran while one was open for 6% -> 0% of each run, Pallas kernels for 0% -> 0%
where the time goes in v2:
time: 158 us
  Pallas kernels  151 us (96%)
  local copies, waits for them, and re-layouts  4.13 us (3%)
    pallas_call x1, Pallas kernels, power_step(): pl.pallas_call(power_kernel, name='power_step', out_shape=[jax.ShapeDtype...  151 us
    unnamed x2, local copies, waits for them, and re-layouts  4.13 us

profile of v2, /device:TPU:1, one launch (start us, length us, event | category | flops | bytes accessed | tf_op | source)
XLA Modules:
  0.0 158.1 jit_solution(177637138456284920)
XLA Ops:
  1.3 0.7 add_bitcast_fusion
  2.0 0.6 select_reduce_fusion.slot_ref
  2.6 151.4 %power_step.1 = (f32[256,512]{1,0:T(8,128)}, f32[512,512]{1,0:T(8,128)}) custom-call(s32[64]{0:T(128)} %select_reduce_fusion.slot_ref, bf16[32,256,256]{2,1,0:T(8,128)(2,1)} %bitcast.5, bf16[256,512]{1,0:T(8,128)(2,1)} %sketch_ref.1), custom_call_target="tpu_custom_call" | custom-call | tf_op jit(solution)/shard_map/power_step/pallas_call | solution.py:540
  153.9 1.9 %copy.10 = f32[256,512]{1,0:T(8,128)} copy(f32[256,512]{1,0:T(8,128)} %get-tuple-element.4) | data formatting | bytes 1048576
  155.8 2.3 %copy.11 = f32[512,512]{1,0:T(8,128)} copy(f32[512,512]{1,0:T(8,128)} %get-tuple-element.5) | data formatting | bytes 2097152
  (1 shorter events, 0.0 us)

commit v3 on v2

--- a/solution.py
+++ b/solution.py
@@ -98,6 +98,7 @@
     E[:] = [(lid == rid + 8 * i).astype(F32) for i in range(16)]
     for g in range(16):
         cols = [lane(S[g], 8 * g + k) for k in range(8)]
+        ss, ee = [sub(S[g], k) for k in range(8)], [sub(E[g], k) for k in range(8)]
         a = {(i, k): sub(cols[k], i) for k in range(8) for i in range(k, 8)}
         r, l, m = [None] * 8, {}, {}
         for k in range(8):
@@ -107,31 +108,30 @@
             for i in range(k + 1, 8):
                 for n in range(k + 1, i + 1):
                     a[i, n] = a[i, n] - l[i, k] * l[n, k]
-        for j in range(8):
-            m[j, j] = r[j]
-            for i in range(j + 1, 8):
-                t = l[i, j] * m[j, j]
-                for k in range(j + 1, i):
-                    t = t + l[i, k] * m[k, j]
-                m[i, j] = -(t * r[i])
-        u = e = None
-        for k in range(8):
-            c = jnp.zeros((8, 128), F32)
-            for i in range(k, 8):
-                c = jnp.where(rid == i, m[i, k], c)
-            tu, te = c * sub(S[g], k), c * sub(E[g], k)
-            u, e = (tu, te) if u is None else (u + tu, e + te)
-        S[g], E[g] = u, e
-        if g < 15:
-            us, es = [sub(u, k) for k in range(8)], [sub(e, k) for k in range(8)]
-            turned = u.T
-            for i in range(g + 1, 16):
-                c = turned[8 * i:8 * i + 8, :]
-                for k in range(8):
-                    ck = jnp.broadcast_to(c[:, k:k + 1], (8, 128))
-                    S[i] = S[i] - ck * us[k]
-                    E[i] = E[i] - ck * es[k]
-            yield CHOL
+            m[k, k] = r[k]
+            for j in range(k):
+                t = l[k, j] * m[j, j]
+                for q in range(j + 1, k):
+                    t = t + l[k, q] * m[q, j]
+                m[k, j] = -(t * r[k])
+
+        def mixed(terms, n):
+            value = terms[0] * m[n, 0]
+            for k in range(1, n + 1):
+                value = value + terms[k] * m[n, k]
+            return value
+
+        us, es = [mixed(ss, n) for n in range(8)], [mixed(ee, n) for n in range(8)]
+        later = {i: [lane(S[i], 8 * g + k) for k in range(8)] for i in range(g + 1, 16)}
+        for i in range(g + 1, 16):
+            for n in range(8):
+                c = mixed(later[i], n)
+                S[i] = S[i] - c * us[n]
+                E[i] = E[i] - c * es[n]
+        S[g], E[g] = us[0], es[0]
+        for n in range(1, 8):
+            S[g], E[g] = jnp.where(rid == n, us[n], S[g]), jnp.where(rid == n, es[n], E[g])
+        yield CHOL
     S[:] = [jnp.where(lid >= rid + 8 * i, s, 0.0) for i, s in enumerate(S)]
 
 
@@ -350,10 +350,12 @@
         for dq in QS:
             for h in range(2):
                 send1(h, 2, dq, via(dq), product(h, 2, dq))
+            yield PROD
         for dq in QS:
             for h in range(2):
                 s = -via(dq)
                 send1(h, s, dq, s, product(h, s, dq))
+            yield PROD
         for dq in QS:
             for h in range(2):
                 product(h, via(dq), dq)
@@ -409,7 +411,7 @@
         half, quarter, first, second = size // 2, size // 4, size // 16, size // 64
         base = pl.multiple_of(net.c * half, 256)
         twin = start(net.copy(gbuf.at[pl.ds(pl.multiple_of((1 - net.c) * half, 256), half), :], gpair.at[pl.ds(t * 256, half), :], dc=1))
-        yield GM1
+        yield GM1[t]
         twin.wait_recv()
         gbuf[pl.ds(base, half), :] += gpair[t * 256:t * 256 + half, :]
 
@@ -426,7 +428,7 @@
                     land = g1.at[t, v, n, pl.ds(0, step), :] if level == 0 else g2.at[t, v, n, pl.ds(0, step), :]
                     axis = axes[v][level]
                     copies[v, n] = start(net.copy(gbuf.at[cut(ats[v], place[(v + level) % 2], d, step), :], land, **{axis: d}))
-            yield GM2
+            yield GM2[t]
             for v in range(2):
                 here = cut(ats[v], place[(v + level) % 2], 0, step)
                 value = gbuf[here, :]
@@ -442,7 +444,7 @@
         offsets = (4, 3, -3, 2, -2, 1, -1, 0)
         copies = [start(net.copy(gstage.at[t, pl.ds(0, both), :], gz.at[t, n, pl.ds(0, both), :], dz=d)) for n, d in enumerate(offsets[:-1])]
         gz[t, 7, 0:both, :] = gstage[t, 0:both, :]
-        yield GM3
+        yield GM3[t]
         for copy in copies:
             copy.wait_recv()
         value = None
@@ -463,12 +465,12 @@
                 where = out.at[pl.ds(pl.multiple_of(ats[v], 8), step), :]
                 for d in (2, 1, -1):
                     copies.append(start(net.copy(where, where, **{axes[v][level]: d})))
-            yield GM2
+            yield GM2[t]
             for copy in copies:
                 copy.wait_recv()
         where = out.at[pl.ds(base, half), :]
         twin = start(net.copy(where, where, dc=1))
-        yield GM1
+        yield GM1[t]
         twin.wait_recv()
 
     index = {p: n for n, p in enumerate(PANELS)}
@@ -527,12 +529,13 @@
         copy.wait_send()
 
 
-SECOND = 15.0
-GATHER = ((8.0, 1.0), (5.0, 1.2))
-ZPAIR, ZFAR, ZNEAR, ZLAST, ZRING, ZSHARE = 3.0, 4.5, 1.0, 3.0, 3.5, 1.5
-RS1, RS2, RS3, RS4 = (4.0, 1.2, 1.2, 1.2), (2.5, 1.2, 1.2, 1.2), (1.5, 0.7), 2.5
-GM1, GM2, GM3 = 2.0, 3.0, 6.0
-CHOL = 0.45
+SECOND = 20.0
+GATHER = ((9.0, 1.1), (5.0, 1.3))
+ZPAIR, ZFAR, ZNEAR, ZLAST, ZRING, ZSHARE = 3.5, 6.5, 1.0, 5.0, 4.5, 2.0
+PROD = 0.6
+RS1, RS2, RS3, RS4 = (0.6, 1.2, 1.2, 1.2), (2.5, 1.2, 1.2, 1.2), (1.5, 0.7), 2.5
+GM1, GM2, GM3 = (3.0, 2.0), (4.5, 3.0), (6.5, 6.0)
+CHOL = 0.4
 
 
 def power_step(slots, tiles, sketch):
@@ -576,11 +579,32 @@
     )(slots, tiles, sketch)
 
 
+def hand_kernel(basis, factor, basis_out, factor_out, sems):
+    copies = [pltpu.make_async_copy(basis.at[pl.ds(128 * n, 128), :], basis_out.at[pl.ds(128 * n, 128), :], sems.at[n]) for n in range(2)]
+    copies += [pltpu.make_async_copy(factor.at[pl.ds(128 * n, 128), :], factor_out.at[pl.ds(128 * n, 128), :], sems.at[2 + n]) for n in range(4)]
+    for copy in copies:
+        copy.start()
+    for copy in copies:
+        copy.wait()
+
+
+def hand_over(basis, factor):
+    anywhere = pl.BlockSpec(memory_space=pl.ANY)
+    return pl.pallas_call(
+        hand_kernel,
+        name="hand_over",
+        out_shape=[jax.ShapeDtypeStruct((EDGE, K), F32), jax.ShapeDtypeStruct((K, K), F32)],
+        in_specs=[anywhere, anywhere],
+        out_specs=[anywhere, anywhere],
+        scratch_shapes=[pltpu.SemaphoreType.DMA((6,))],
+        compiler_params=pltpu.CompilerParams(vmem_limit_bytes=60 << 20),
+    )(basis, factor)
+
+
 def local(tiles, tile_rows, tile_cols, counts, sketch):
     blocks = tiles[0, 0]
     slots = slot_table(tile_rows[0, 0], tile_cols[0, 0], counts[0, 0])
-    basis, factor = power_step(slots, blocks, sketch)
-    return basis, factor
+    return hand_over(*power_step(slots, blocks, sketch))
 
 
 def solution(mesh):

time: 158 us -> 189 us (1.20)
  Pallas kernels: 151 us -> 186 us
  local copies, waits for them, and re-layouts: 4.13 us -> 0 us
    pallas_call x0 -> x1, Pallas kernels: none -> 48.8 us  [hand_over(): pl.pallas_call(hand_kernel, name='hand_over', out_shape=[jax.ShapeDtypeSt...]
    pallas_call x1, Pallas kernels: 151 us -> 138 us  [power_step(): pl.pallas_call(power_kernel, name='power_step', out_shape=[jax.ShapeDtype...]
    unnamed x2 -> x0, local copies, waits for them, and re-layouts: 4.13 us -> none
where the time goes in v3:
time: 189 us
  Pallas kernels  186 us (98%)
    pallas_call x1, Pallas kernels, power_step(): pl.pallas_call(power_kernel, name='power_step', out_shape=[jax.ShapeDtype...  138 us
    pallas_call x1, Pallas kernels, hand_over(): pl.pallas_call(hand_kernel, name='hand_over', out_shape=[jax.ShapeDtypeSt...  48.8 us

profile of v3, /device:TPU:1, one launch (start us, length us, event | category | flops | bytes accessed | tf_op | source)
XLA Modules:
  0.0 189.3 jit_solution(7669234467021938804)
XLA Ops:
  1.3 0.7 add_bitcast_fusion
  2.0 0.6 select_reduce_fusion.slot_ref
  2.6 137.7 %power_step.1 = (f32[256,512]{1,0:T(8,128)}, f32[512,512]{1,0:T(8,128)}) custom-call(s32[64]{0:T(128)} %select_reduce_fusion.slot_ref, bf16[32,256,256]{2,1,0:T(8,128)(2,1)} %bitcast.5, bf16[256,512]{1,0:T(8,128)(2,1)} %sketch_ref.1), custom_call_target="tpu_custom_call" | custom-call | tf_op jit(solution)/shard_map/power_step/pallas_call | solution.py:543
  140.3 48.8 %hand_over.1 = (f32[256,512]{1,0:T(8,128)}, f32[512,512]{1,0:T(8,128)}) custom-call(f32[256,512]{1,0:T(8,128)} %get-tuple-element.4.basis, f32[512,512]{1,0:T(8,128)} %get-tuple-element.5.factor), custom_call_target="tpu_custom_call" | custom-call | tf_op jit(solution)/shard_map/hand_over/pallas_call | solution.py:593
  (1 shorter events, 0.0 us)

commit v4 on v3

--- a/solution.py
+++ b/solution.py
@@ -579,24 +579,20 @@
     )(slots, tiles, sketch)
 
 
-def hand_kernel(basis, factor, basis_out, factor_out, sems):
-    copies = [pltpu.make_async_copy(basis.at[pl.ds(128 * n, 128), :], basis_out.at[pl.ds(128 * n, 128), :], sems.at[n]) for n in range(2)]
-    copies += [pltpu.make_async_copy(factor.at[pl.ds(128 * n, 128), :], factor_out.at[pl.ds(128 * n, 128), :], sems.at[2 + n]) for n in range(4)]
-    for copy in copies:
-        copy.start()
-    for copy in copies:
-        copy.wait()
+def hand_kernel(basis, factor, basis_out, factor_out):
+    basis_out[...] = basis[...]
+    factor_out[...] = factor[...]
 
 
 def hand_over(basis, factor):
-    anywhere = pl.BlockSpec(memory_space=pl.ANY)
+    specs = [pl.BlockSpec((EDGE // 4, K), lambda n: (n, 0)), pl.BlockSpec((K // 4, K), lambda n: (n, 0))]
     return pl.pallas_call(
         hand_kernel,
         name="hand_over",
+        grid=(4,),
         out_shape=[jax.ShapeDtypeStruct((EDGE, K), F32), jax.ShapeDtypeStruct((K, K), F32)],
-        in_specs=[anywhere, anywhere],
-        out_specs=[anywhere, anywhere],
-        scratch_shapes=[pltpu.SemaphoreType.DMA((6,))],
+        in_specs=specs,
+        out_specs=specs,
         compiler_params=pltpu.CompilerParams(vmem_limit_bytes=60 << 20),
     )(basis, factor)
 

time: 189 us -> 144 us (0.76)
  Pallas kernels: 186 us -> 141 us
    pallas_call x1, Pallas kernels: 48.8 us -> 3.62 us  [hand_over(): pl.pallas_call(hand_kernel, name='hand_over', grid=(4,), out_shape=[jax.S...]
where the time goes in v4:
time: 144 us
  Pallas kernels  141 us (98%)
    pallas_call x1, Pallas kernels, power_step(): pl.pallas_call(power_kernel, name='power_step', out_shape=[jax.ShapeDtype...  138 us
    pallas_call x1, Pallas kernels, hand_over(): pl.pallas_call(hand_kernel, name='hand_over', grid=(4,), out_shape=[jax.S...  3.62 us

profile of v4, /device:TPU:1, one launch (start us, length us, event | category | flops | bytes accessed | tf_op | source)
XLA Modules:
  0.0 143.9 jit_solution(1689542836793564376)
XLA Ops:
  1.3 0.7 add_bitcast_fusion
  2.0 0.6 select_reduce_fusion.slot_ref
  2.6 137.7 %power_step.1 = (f32[256,512]{1,0:T(8,128)}, f32[512,512]{1,0:T(8,128)}) custom-call(s32[64]{0:T(128)} %select_reduce_fusion.slot_ref, bf16[32,256,256]{2,1,0:T(8,128)(2,1)} %bitcast.5, bf16[256,512]{1,0:T(8,128)(2,1)} %sketch_ref.1), custom_call_target="tpu_custom_call" | custom-call | tf_op jit(solution)/shard_map/power_step/pallas_call | solution.py:543
  140.3 3.6 %hand_over.1 = (f32[256,512]{1,0:T(8,128)}, f32[512,512]{1,0:T(8,128)}) custom-call(f32[256,512]{1,0:T(8,128)} %get-tuple-element.4.basis, f32[512,512]{1,0:T(8,128)} %get-tuple-element.5.factor), custom_call_target="tpu_custom_call" | custom-call | tf_op jit(solution)/shard_map/hand_over/pallas_call | solution.py:589
  (1 shorter events, 0.0 us)

commit v5 on v4

--- a/solution.py
+++ b/solution.py
@@ -529,7 +529,7 @@
         copy.wait_send()
 
 
-SECOND = 20.0
+SECOND = 23.0
 GATHER = ((9.0, 1.1), (5.0, 1.3))
 ZPAIR, ZFAR, ZNEAR, ZLAST, ZRING, ZSHARE = 3.5, 6.5, 1.0, 5.0, 4.5, 2.0
 PROD = 0.6

time: 144 us -> 142 us (0.986)
    pallas_call x1, Pallas kernels: 138 us -> 136 us  [power_step(): pl.pallas_call(power_kernel, name='power_step', out_shape=[jax.ShapeDtype...]
where the time goes in v5:
time: 142 us
  Pallas kernels  140 us (99%)
    pallas_call x1, Pallas kernels, power_step(): pl.pallas_call(power_kernel, name='power_step', out_shape=[jax.ShapeDtype...  136 us
    pallas_call x1, Pallas kernels, hand_over(): pl.pallas_call(hand_kernel, name='hand_over', grid=(4,), out_shape=[jax.S...  3.62 us

profile of v5, /device:TPU:1, one launch (start us, length us, event | category | flops | bytes accessed | tf_op | source)
XLA Modules:
  0.0 142.2 jit_solution(1429403720600135695)
XLA Ops:
  1.3 0.7 add_bitcast_fusion
  2.0 0.6 select_reduce_fusion.slot_ref
  2.6 136.0 %power_step.1 = (f32[256,512]{1,0:T(8,128)}, f32[512,512]{1,0:T(8,128)}) custom-call(s32[64]{0:T(128)} %select_reduce_fusion.slot_ref, bf16[32,256,256]{2,1,0:T(8,128)(2,1)} %bitcast.5, bf16[256,512]{1,0:T(8,128)(2,1)} %sketch_ref.1), custom_call_target="tpu_custom_call" | custom-call | tf_op jit(solution)/shard_map/power_step/pallas_call | solution.py:543
  138.6 3.6 %hand_over.1 = (f32[256,512]{1,0:T(8,128)}, f32[512,512]{1,0:T(8,128)}) custom-call(f32[256,512]{1,0:T(8,128)} %get-tuple-element.4.basis, f32[512,512]{1,0:T(8,128)} %get-tuple-element.5.factor), custom_call_target="tpu_custom_call" | custom-call | tf_op jit(solution)/shard_map/hand_over/pallas_call | solution.py:589
  (1 shorter events, 0.0 us)
